TPU v7x, 1024 devices: a whole 4x8x16 slice. The times are simulated.
1024 devices in a mesh: replica: 64 (over z, y_hi, core), tensor: 16 (over y_lo, x).
Axes of the slice: x: 4, y: 8 (y_hi: 2, y_lo: 4; y = y_hi * 4 + y_lo), z: 16, core: 2. Of those that a mesh axis runs over, the one named last changes fastest.
Arguments:
- queries: bfloat16 [4096, 8192], P(('replica', 'tensor')), may hold values from -64 to 64
- stored_keys: bfloat16 [4096, 8, 128, 128], P(('replica', 'tensor')), may hold values from -4 to 4
- stored_values: bfloat16 [4096, 8, 128, 128], P(('replica', 'tensor')), may hold values from -6 to 6
- lengths: int32 [4096], P(('replica', 'tensor')), may hold values from 1 to 128
- hidden: bfloat16 [4096, 5120], P(('replica', 'tensor')), may hold values from -3 to 3
- output_weight: bfloat16 [8192, 5120], P('tensor'), may hold values from -0.0625 to 0.0625
- adapter_down: bfloat16 [128, 8192], P('replica', 'tensor'), may hold values from -0.0625 to 0.0625
- adapter_up: bfloat16 [128, 5120], P('replica', 'tensor'), may hold values from -0.5 to 0.5
Outputs:
- block_out: bfloat16 [4096, 5120], P(('replica', 'tensor'))
All inputs are finite; a program needn't handle non-finite values.
Results may differ from a plain program's by a relative error of at most 0.007.
Values may be sent and summed in bfloat16 or wider, within the bound.
No kernel may reach another device: no remote copies, remote signals or barrier semaphores. Data moves between devices by JAX's collectives and lax.ppermute only.
A program may use at most 32 MiB of HBM per device.

v0:
```python
import math

import jax
import jax.numpy as jnp
from jax import lax
from jax.sharding import PartitionSpec as P

QUERY_HEADS = 64
KVH = 8
HEAD_SIZE = 128
CACHE = 128
GROUP = 8
N_TENSOR = 16
N_REPLICA = 64

adapter_scale = 2.0

HALF = 8
PLACE_GROUPS = [[half * HALF + near for near in range(HALF) for half in range(2)]]
HALF_GROUPS = [[upper * HALF + near for near in range(HALF)] for upper in range(2)]
DEPTH = 16
Z_GROUPS = [[z * 4 + rest for z in range(DEPTH)] for rest in range(4)]


def attend_rows(queries, stored_keys, stored_values, lengths):
    row_count = queries.shape[0]
    shaped = queries.reshape(row_count, KVH, GROUP, HEAD_SIZE)
    scores = jnp.einsum(
        "rkgd,rksd->rkgs", shaped, stored_keys, preferred_element_type=jnp.float32
    ) / math.sqrt(HEAD_SIZE)
    positions = jnp.arange(CACHE, dtype=jnp.int32)
    visible = positions[None, :] < lengths[:, None]
    scores = jnp.where(visible[:, None, None, :], scores, -1e30)
    highest = jnp.max(scores, axis=-1, keepdims=True)
    expo = jnp.exp(scores - highest)
    denominator = jnp.sum(expo, axis=-1, keepdims=True)
    probs = (expo / denominator).astype(jnp.bfloat16)
    attended = jnp.einsum(
        "rkgs,rksd->rkgd", probs, stored_values, preferred_element_type=jnp.float32
    )
    return attended.astype(jnp.bfloat16).reshape(row_count, QUERY_HEADS * HEAD_SIZE)


def spread(block, axis, count, groups=None):
    copies = jnp.broadcast_to(block[None], (count,) + block.shape)
    return lax.all_to_all(copies, axis, 0, 0, axis_index_groups=groups)


def swap(block, axis, count, bit):
    return lax.ppermute(block, axis, [(i, i ^ bit) for i in range(count)])


def gather_along_z(adapter_down, adapter_up):
    both = jnp.concatenate([adapter_down, adapter_up], axis=1)
    rank, width = both.shape
    return spread(both, "replica", DEPTH, Z_GROUPS).reshape(DEPTH * rank, width)


def gather_rest(some, split):
    for bit in (2, 1):
        other = swap(some, "replica", N_REPLICA, bit)
        some = jnp.concatenate([some, other], axis=0)
    return some[:, :split], some[:, split:]


def per_device(
    queries, stored_keys, stored_values, lengths, hidden, output_weight, adapter_down, adapter_up
):
    rows, width = hidden.shape
    some = gather_along_z(adapter_down, adapter_up)
    attended = attend_rows(queries, stored_keys, stored_values, lengths)
    blocks = attended.reshape(rows, 2, HALF, -1).transpose(2, 1, 0, 3)
    blocks = blocks.reshape(N_TENSOR, rows, -1)
    some, blocks = lax.optimization_barrier((some, blocks))
    down, up = gather_rest(some, adapter_down.shape[1])
    grouped = lax.all_to_all(blocks, "tensor", 0, 0, axis_index_groups=PLACE_GROUPS)
    grouped = grouped.reshape(N_TENSOR * rows, -1)

    low_part = lax.dot_general(
        down, grouped, (((1,), (1,)), ((), ())), preferred_element_type=jnp.float32
    ).astype(jnp.bfloat16)
    by_rank = jnp.concatenate([low_part, up], axis=1)
    by_rank = lax.all_to_all(by_rank.reshape(N_TENSOR, -1, by_rank.shape[1]), "tensor", 0, 0)
    partial_value = jnp.dot(grouped, output_weight, preferred_element_type=jnp.float32)
    residual, upper, by_rank = lax.optimization_barrier(
        (hidden.astype(jnp.float32), lax.axis_index("tensor") >= HALF, by_rank)
    )
    low = jnp.sum(by_rank[:, :, : N_TENSOR * rows].astype(jnp.float32), axis=0)
    up = by_rank[:, :, N_TENSOR * rows :].transpose(1, 0, 2).reshape(-1, width)
    delta = lax.dot_general(
        low.astype(jnp.bfloat16), up, (((0,), (0,)), ((), ())), preferred_element_type=jnp.float32
    )
    partial_value = (partial_value + adapter_scale * delta).astype(jnp.bfloat16)
    received = lax.all_to_all(
        partial_value.reshape(HALF, 2 * rows, width),
        "tensor",
        0,
        0,
        axis_index_groups=HALF_GROUPS,
    )
    reduced = jnp.sum(received.astype(jnp.float32), axis=0)
    kept = jnp.where(upper, reduced[rows:], reduced[:rows])
    sent = jnp.where(upper, reduced[:rows], reduced[rows:]).astype(jnp.bfloat16)
    other = swap(sent, "tensor", N_TENSOR, HALF)
    return (residual + kept + other.astype(jnp.float32)).astype(jnp.bfloat16)


def solution(mesh):
    in_specs = (
        P(("replica", "tensor"), None),
        P(("replica", "tensor"), None, None, None),
        P(("replica", "tensor"), None, None, None),
        P(("replica", "tensor")),
        P(("replica", "tensor"), None),
        P("tensor", None),
        P("replica", "tensor"),
        P("replica", "tensor"),
    )
    out_specs = P(("replica", "tensor"), None)
    return jax.shard_map(
        per_device, mesh=mesh, in_specs=in_specs, out_specs=out_specs, check_vma=False
    )
```

profile of v0, /device:TPU:8, one launch (start us, length us, event | category | flops | bytes accessed | tf_op | source)
XLA Modules:
  0.0 86.6 jit_solution(10137952815573557963)
XLA Ops:
  0.0 0.9 pad_maximum_fusion.1
  0.9 0.6 broadcast_in_dim.10
  1.5 18.9 %all-to-all-start = ((bf16[16,2,832]{2,1,0:T(2,128)(2,1)}), bf16[16,2,832]{2,1,0:T(2,128)(2,1)S(1)}, u32[]{:S(2)}, u32[]{:S(2)}) async-start(bf16[16,2,832]{2,1,0:T(2,128)(2,1)} %broadcast_in_dim.10), calls=%async_computation | async-start | bytes 114688 | tf_op jit(solution)/shard_map/all_to_all | solution.py:46
  20.4 0.7 iota_compare_fusion
  21.1 0.8 convert_element_type.29
  21.9 1.5 %fusion.6 = f32[4,8,8,128]{3,2,1,0:T(8,128)S(1)} fusion(bf16[4,8,128,128]{3,2,1,0:T(8,128)(2,1)S(1)} %copy-done, bf16[1,4,64,128]{3,1,2,0:T(4,128)(2,1)} %bitcast.25, pred[4,128]{1,0:T(4,128)(4,1)S(1)} %iota_compare_fusion), kind=kOutput, calls=%fused_computation.9 | convolution fusion | flops 8454144 | bytes 1245696 | tf_op jit(solution)/shard_map/rkgd,rksd->rkgs/dot_general | solution.py:28
  23.4 0.2 fusion.11
  23.6 0.6 convolution_convert_fusion
  24.2 0.1 reshape_reshape.3
  24.3 0.7 copy.12
  24.9 8.1 %all-to-all-done = bf16[16,2,832]{2,1,0:T(2,128)(2,1)S(1)} async-done(((bf16[16,2,832]{2,1,0:T(2,128)(2,1)}), bf16[16,2,832]{2,1,0:T(2,128)(2,1)S(1)}, u32[]{:S(2)}, u32[]{:S(2)}) %all-to-all-start) | async-done | bytes 53280 | tf_op jit(solution)/shard_map/all_to_all | solution.py:46
  33.1 0.1 reshape.41
  33.1 6.8 %collective-permute-start = (bf16[32,832]{1,0:T(8,128)(2,1)S(1)}, bf16[32,832]{1,0:T(8,128)(2,1)S(1)}, u32[]{:S(2)}, u32[]{:S(2)}) collective-permute-start(bf16[32,832]{1,0:T(8,128)(2,1)S(1)} %reshape.41), channel_id=1, source_target_pairs={{0,32},{16,48},{32,0},{48,16},{64,96},{80,112},{96,64},{112,80},{1... | collective-permute-start | bytes 159752 | tf_op jit(solution)/shard_map/ppermute | solution.py:50
  40.0 6.0 %all-to-all-start.1 = ((bf16[16,4,512]{2,1,0:T(4,128)(2,1)}), bf16[16,4,512]{2,1,0:T(4,128)(2,1)S(1)}, u32[]{:S(2)}, u32[]{:S(2)}) async-start(bf16[16,4,512]{2,1,0:T(4,128)(2,1)} %bitcast.1), calls=%async_computation.1 | async-start | bytes 131072 | tf_op jit(solution)/shard_map/all_to_all | solution.py:76
  46.0 0.0 collective-permute-done
  46.0 1.9 %collective-permute-start.1 = (bf16[64,832]{1,0:T(8,128)(2,1)S(1)}, bf16[64,832]{1,0:T(8,128)(2,1)S(1)}, u32[]{:S(2)}, u32[]{:S(2)}) collective-permute-start(bf16[64,832]{1,0:T(8,128)(2,1)S(1)} %pad_maximum_fusion), channel_id=1, source_target_pairs={{0,16},{16,0},{32,48},{48,32},{64,80},{80,64},{96,112},{112,96},{1... | collective-permute-start | bytes 319496 | tf_op jit(solution)/shard_map/ppermute | solution.py:50
  48.0 5.0 %all-to-all-done.1 = bf16[16,4,512]{2,1,0:T(4,128)(2,1)S(1)} async-done(((bf16[16,4,512]{2,1,0:T(4,128)(2,1)}), bf16[16,4,512]{2,1,0:T(4,128)(2,1)S(1)}, u32[]{:S(2)}, u32[]{:S(2)}) %all-to-all-start.1) | async-done | bytes 65568 | tf_op jit(solution)/shard_map/all_to_all | solution.py:76
  53.0 0.0 collective-permute-done.1
  53.0 0.2 convolution_convert_fusion.1
  53.2 0.1 copy.13
  53.3 0.7 maximum_bitcast_fusion
  54.0 4.6 %all-to-all-start.2 = ((bf16[16,8,384]{2,1,0:T(8,128)(2,1)}), bf16[16,8,384]{2,1,0:T(8,128)(2,1)S(1)}, u32[]{:S(2)}, u32[]{:S(2)}) async-start(bf16[16,8,384]{2,1,0:T(8,128)(2,1)} %maximum_bitcast_fusion), calls=%async_computation.2 | async-start | bytes 196608 | tf_op jit(solution)/shard_map/all_to_all | solution.py:83
  58.6 3.5 %fusion.12 = f32[64,5120]{1,0:T(8,128)S(1)} fusion(bf16[64,512]{1,0:T(8,128)(2,1)S(1)} %reshape.44, bf16[512,5120]{1,0:T(8,128)(2,1)} %param.13), kind=kOutput, calls=%fused_computation.29 | convolution fusion | flops 335544320 | bytes 6619136 | tf_op jit(solution)/shard_map/dot_general | solution.py:84
  62.2 3.3 %all-to-all-done.2 = bf16[16,8,384]{2,1,0:T(8,128)(2,1)S(1)} async-done(((bf16[16,8,384]{2,1,0:T(8,128)(2,1)}), bf16[16,8,384]{2,1,0:T(8,128)(2,1)S(1)}, u32[]{:S(2)}, u32[]{:S(2)}) %all-to-all-start.2) | async-done | bytes 98336 | tf_op jit(solution)/shard_map/all_to_all | solution.py:83
  65.5 0.1 slice_bitcast_fusion
  65.6 0.1 reshape.46
  65.7 0.4 fusion.3
  66.1 12.8 %all_to_all.20 = bf16[8,8,5120]{2,1,0:T(8,128)(2,1)S(1)} all-to-all(bf16[8,8,5120]{2,1,0:T(8,128)(2,1)S(1)} %fusion.3), channel_id=1, replica_groups={{0,1,2,3,4,5,6,7},{8,9,10,11,12,13,14,15},{16,17,18,19,20,21,22,23},{24..., dimensions={0} | all-to-all | bytes 1310720 | tf_op jit(solution)/shard_map/all_to_all | solution.py:94
  78.9 0.1 convert_reduce_fusion
  79.1 2.7 %collective-permute-start.2 = (bf16[4,5120]{1,0:T(4,128)(2,1)S(1)}, bf16[4,5120]{1,0:T(4,128)(2,1)S(1)}, u32[]{:S(2)}, u32[]{:S(2)}) collective-permute-start(bf16[4,5120]{1,0:T(4,128)(2,1)S(1)} %select_convert_fusion), channel_id=1, source_target_pairs={{0,8},{1,9},{2,10},{3,11},{4,12},{5,13},{6,14},{7,15},{8,0},{9,1},... | collective-permute-start | bytes 122888 | tf_op jit(solution)/shard_map/ppermute | solution.py:50
  81.8 4.2 %collective-permute-done.2 = bf16[4,5120]{1,0:T(4,128)(2,1)S(1)} collective-permute-done((bf16[4,5120]{1,0:T(4,128)(2,1)S(1)}, bf16[4,5120]{1,0:T(4,128)(2,1)S(1)}, u32[]{:S(2)}, u32[]{:S(2)}) %collective-permute-start.2) | collective-permute-done | bytes 40992 | tf_op jit(solution)/shard_map/ppermute | solution.py:50
  86.0 0.7 add_convert_fusion
  (13 shorter events, 0.2 us)
Async XLA Ops:
  0.0 21.9 %copy-start = (bf16[4,8,128,128]{3,2,1,0:T(8,128)(2,1)S(1)}, bf16[4,8,128,128]{3,2,1,0:T(8,128)(2,1)}, u32[]{:S(2)}) copy-start(bf16[4,8,128,128]{3,2,1,0:T(8,128)(2,1)} %param.9) | copy-start | bytes 3145732
  0.0 23.6 %copy-start.1 = (bf16[4,8,128,128]{3,2,1,0:T(8,128)(2,1)S(1)}, bf16[4,8,128,128]{3,2,1,0:T(8,128)(2,1)}, u32[]{:S(2)}) copy-start(bf16[4,8,128,128]{3,2,1,0:T(8,128)(2,1)} %param.10) | copy-start | bytes 3145732
  1.5 31.6 %all-to-all-start = ((bf16[16,2,832]{2,1,0:T(2,128)(2,1)}), bf16[16,2,832]{2,1,0:T(2,128)(2,1)S(1)}, u32[]{:S(2)}, u32[]{:S(2)}) async-start(bf16[16,2,832]{2,1,0:T(2,128)(2,1)} %broadcast_in_dim.10), calls=%async_computation | async-start | bytes 114688 | tf_op jit(solution)/shard_map/all_to_all | solution.py:46
  33.1 12.9 %collective-permute-start = (bf16[32,832]{1,0:T(8,128)(2,1)S(1)}, bf16[32,832]{1,0:T(8,128)(2,1)S(1)}, u32[]{:S(2)}, u32[]{:S(2)}) collective-permute-start(bf16[32,832]{1,0:T(8,128)(2,1)S(1)} %reshape.41), channel_id=1, source_target_pairs={{0,32},{16,48},{32,0},{48,16},{64,96},{80,112},{96,64},{112,80},{1... | collective-permute-start | bytes 159752 | tf_op jit(solution)/shard_map/ppermute | solution.py:50
  40.0 13.0 %all-to-all-start.1 = ((bf16[16,4,512]{2,1,0:T(4,128)(2,1)}), bf16[16,4,512]{2,1,0:T(4,128)(2,1)S(1)}, u32[]{:S(2)}, u32[]{:S(2)}) async-start(bf16[16,4,512]{2,1,0:T(4,128)(2,1)} %bitcast.1), calls=%async_computation.1 | async-start | bytes 131072 | tf_op jit(solution)/shard_map/all_to_all | solution.py:76
  46.0 6.9 %collective-permute-start.1 = (bf16[64,832]{1,0:T(8,128)(2,1)S(1)}, bf16[64,832]{1,0:T(8,128)(2,1)S(1)}, u32[]{:S(2)}, u32[]{:S(2)}) collective-permute-start(bf16[64,832]{1,0:T(8,128)(2,1)S(1)} %pad_maximum_fusion), channel_id=1, source_target_pairs={{0,16},{16,0},{32,48},{48,32},{64,80},{80,64},{96,112},{112,96},{1... | collective-permute-start | bytes 319496 | tf_op jit(solution)/shard_map/ppermute | solution.py:50
  54.0 11.4 %all-to-all-start.2 = ((bf16[16,8,384]{2,1,0:T(8,128)(2,1)}), bf16[16,8,384]{2,1,0:T(8,128)(2,1)S(1)}, u32[]{:S(2)}, u32[]{:S(2)}) async-start(bf16[16,8,384]{2,1,0:T(8,128)(2,1)} %maximum_bitcast_fusion), calls=%async_computation.2 | async-start | bytes 196608 | tf_op jit(solution)/shard_map/all_to_all | solution.py:83
  79.1 6.9 %collective-permute-start.2 = (bf16[4,5120]{1,0:T(4,128)(2,1)S(1)}, bf16[4,5120]{1,0:T(4,128)(2,1)S(1)}, u32[]{:S(2)}, u32[]{:S(2)}) collective-permute-start(bf16[4,5120]{1,0:T(4,128)(2,1)S(1)} %select_convert_fusion), channel_id=1, source_target_pairs={{0,8},{1,9},{2,10},{3,11},{4,12},{5,13},{6,14},{7,15},{8,0},{9,1},... | collective-permute-start | bytes 122888 | tf_op jit(solution)/shard_map/ppermute | solution.py:50
where the time goes:
time: 87.2 us; the launch traced here: 86.6 us
  starting transfers between devices  41 us (47%)
  waiting for transfers between devices  20.6 us (24%)
  blocking collectives  12.8 us (15%)
  matrix products  6.07 us (7%)
  other arithmetic  4.14 us (5%)
  local copies, waits for them, and re-layouts  1.86 us (2%)
    all_to_all x1, starting transfers between devices, spread(): return lax.all_to_all(copies, axis, 0, 0, axis_index_groups=groups)  18.9 us
    all_to_all x1, blocking collectives, per_device(): lax.all_to_all(partial_value.reshape(HALF, 2 * rows, width), 'tensor', 0,...  12.8 us
    ppermute x3, starting transfers between devices, swap(): return lax.ppermute(block, axis, [(i, i ^ bit) for i in range(count)])  11.5 us
    all_to_all x1, waiting for transfers between devices, spread(): return lax.all_to_all(copies, axis, 0, 0, axis_index_groups=groups)  8.14 us
    all_to_all x1, starting transfers between devices, per_device(): lax.all_to_all(blocks, 'tensor', 0, 0, axis_index_groups=PLACE_GROUPS)  6.02 us
    all_to_all x1, waiting for transfers between devices, per_device(): lax.all_to_all(blocks, 'tensor', 0, 0, axis_index_groups=PLACE_GROUPS)  4.97 us
    all_to_all x1, starting transfers between devices, per_device(): lax.all_to_all(by_rank.reshape(N_TENSOR, -1, by_rank.shape[1]), 'tensor',...  4.6 us
    ppermute x3, waiting for transfers between devices, swap(): return lax.ppermute(block, axis, [(i, i ^ bit) for i in range(count)])  4.16 us
  transfers between devices with their start and end apart: 6, of which 4 were waited for; matrix products, arithmetic and copies ran while one was open for 9% of the time, Pallas kernels for 0%

commit v1 on v0

--- a/solution.py
+++ b/solution.py
@@ -75,6 +75,7 @@
     down, up = gather_rest(some, adapter_down.shape[1])
     grouped = lax.all_to_all(blocks, "tensor", 0, 0, axis_index_groups=PLACE_GROUPS)
     grouped = grouped.reshape(N_TENSOR * rows, -1)
+    hidden, grouped = lax.optimization_barrier((hidden, grouped))
 
     low_part = lax.dot_general(
         down, grouped, (((1,), (1,)), ((), ())), preferred_element_type=jnp.float32

time: 87.2 us -> 87.2 us (level)
  transfers between devices with their start and end apart: 6 -> 6, of which waited for: 4 -> 4; matrix products, arithmetic and copies ran while one was open for 9% -> 8% of each run, Pallas kernels for 0% -> 0%
where the time goes in v1:
time: 87.2 us; the launch traced here: 86.6 us
  starting transfers between devices  41 us (47%)
  waiting for transfers between devices  21.3 us (24%)
  blocking collectives  12.8 us (15%)
  matrix products  6.08 us (7%)
  other arithmetic  3.36 us (4%)
  local copies, waits for them, and re-layouts  1.86 us (2%)
    all_to_all x1, starting transfers between devices, spread(): return lax.all_to_all(copies, axis, 0, 0, axis_index_groups=groups)  18.9 us
    all_to_all x1, blocking collectives, per_device(): lax.all_to_all(partial_value.reshape(HALF, 2 * rows, width), 'tensor', 0,...  12.8 us
    ppermute x3, starting transfers between devices, swap(): return lax.ppermute(block, axis, [(i, i ^ bit) for i in range(count)])  11.5 us
    all_to_all x1, waiting for transfers between devices, spread(): return lax.all_to_all(copies, axis, 0, 0, axis_index_groups=groups)  8.95 us
    all_to_all x1, starting transfers between devices, per_device(): lax.all_to_all(blocks, 'tensor', 0, 0, axis_index_groups=PLACE_GROUPS)  6.02 us
    all_to_all x1, waiting for transfers between devices, per_device(): lax.all_to_all(blocks, 'tensor', 0, 0, axis_index_groups=PLACE_GROUPS)  4.97 us
    all_to_all x1, starting transfers between devices, per_device(): lax.all_to_all(by_rank.reshape(N_TENSOR, -1, by_rank.shape[1]), 'tensor',...  4.6 us
    ppermute x3, waiting for transfers between devices, swap(): return lax.ppermute(block, axis, [(i, i ^ bit) for i in range(count)])  4.11 us
  transfers between devices with their start and end apart: 6, of which 4 were waited for; matrix products, arithmetic and copies ran while one was open for 8% of the time, Pallas kernels for 0%

profile of v1, /device:TPU:8, one launch (start us, length us, event | category | flops | bytes accessed | tf_op | source)
XLA Modules:
  0.0 86.6 jit_solution(3187402321301446274)
XLA Ops:
  0.0 0.9 pad_maximum_fusion.1
  0.9 0.6 broadcast_in_dim.10
  1.5 18.9 %all-to-all-start = ((bf16[16,2,832]{2,1,0:T(2,128)(2,1)}), bf16[16,2,832]{2,1,0:T(2,128)(2,1)S(1)}, u32[]{:S(2)}, u32[]{:S(2)}) async-start(bf16[16,2,832]{2,1,0:T(2,128)(2,1)} %broadcast_in_dim.10), calls=%async_computation | async-start | bytes 114688 | tf_op jit(solution)/shard_map/all_to_all | solution.py:46
  20.4 0.7 iota_compare_fusion
  21.1 0.0 copy-done
  21.1 1.5 %fusion.6 = f32[4,8,8,128]{3,2,1,0:T(8,128)S(1)} fusion(bf16[4,8,128,128]{3,2,1,0:T(8,128)(2,1)S(1)} %copy-done, bf16[1,4,64,128]{3,1,2,0:T(4,128)(2,1)} %bitcast.25, pred[4,128]{1,0:T(4,128)(4,1)S(1)} %iota_compare_fusion), kind=kOutput, calls=%fused_computation.9 | convolution fusion | flops 8454144 | bytes 1245696 | tf_op jit(solution)/shard_map/rkgd,rksd->rkgs/dot_general | solution.py:28
  22.6 0.2 fusion.11
  22.8 0.6 convolution_convert_fusion
  23.4 0.1 reshape_reshape.3
  23.5 0.7 copy.12
  24.1 8.9 %all-to-all-done = bf16[16,2,832]{2,1,0:T(2,128)(2,1)S(1)} async-done(((bf16[16,2,832]{2,1,0:T(2,128)(2,1)}), bf16[16,2,832]{2,1,0:T(2,128)(2,1)S(1)}, u32[]{:S(2)}, u32[]{:S(2)}) %all-to-all-start) | async-done | bytes 53280 | tf_op jit(solution)/shard_map/all_to_all | solution.py:46
  33.1 0.1 reshape.41
  33.1 6.8 %collective-permute-start = (bf16[32,832]{1,0:T(8,128)(2,1)S(1)}, bf16[32,832]{1,0:T(8,128)(2,1)S(1)}, u32[]{:S(2)}, u32[]{:S(2)}) collective-permute-start(bf16[32,832]{1,0:T(8,128)(2,1)S(1)} %reshape.41), channel_id=1, source_target_pairs={{0,32},{16,48},{32,0},{48,16},{64,96},{80,112},{96,64},{112,80},{1... | collective-permute-start | bytes 159752 | tf_op jit(solution)/shard_map/ppermute | solution.py:50
  40.0 6.0 %all-to-all-start.1 = ((bf16[16,4,512]{2,1,0:T(4,128)(2,1)}), bf16[16,4,512]{2,1,0:T(4,128)(2,1)S(1)}, u32[]{:S(2)}, u32[]{:S(2)}) async-start(bf16[16,4,512]{2,1,0:T(4,128)(2,1)} %bitcast.1), calls=%async_computation.1 | async-start | bytes 131072 | tf_op jit(solution)/shard_map/all_to_all | solution.py:76
  46.0 0.0 collective-permute-done
  46.0 1.9 %collective-permute-start.1 = (bf16[64,832]{1,0:T(8,128)(2,1)S(1)}, bf16[64,832]{1,0:T(8,128)(2,1)S(1)}, u32[]{:S(2)}, u32[]{:S(2)}) collective-permute-start(bf16[64,832]{1,0:T(8,128)(2,1)S(1)} %pad_maximum_fusion), channel_id=1, source_target_pairs={{0,16},{16,0},{32,48},{48,32},{64,80},{80,64},{96,112},{112,96},{1... | collective-permute-start | bytes 319496 | tf_op jit(solution)/shard_map/ppermute | solution.py:50
  48.0 5.0 %all-to-all-done.1 = bf16[16,4,512]{2,1,0:T(4,128)(2,1)S(1)} async-done(((bf16[16,4,512]{2,1,0:T(4,128)(2,1)}), bf16[16,4,512]{2,1,0:T(4,128)(2,1)S(1)}, u32[]{:S(2)}, u32[]{:S(2)}) %all-to-all-start.1) | async-done | bytes 65568 | tf_op jit(solution)/shard_map/all_to_all | solution.py:76
  53.0 0.0 collective-permute-done.1
  53.0 0.2 convolution_convert_fusion.1
  53.2 0.1 copy.13
  53.3 0.7 maximum_bitcast_fusion
  54.0 4.6 %all-to-all-start.2 = ((bf16[16,8,384]{2,1,0:T(8,128)(2,1)}), bf16[16,8,384]{2,1,0:T(8,128)(2,1)S(1)}, u32[]{:S(2)}, u32[]{:S(2)}) async-start(bf16[16,8,384]{2,1,0:T(8,128)(2,1)} %maximum_bitcast_fusion), calls=%async_computation.2 | async-start | bytes 196608 | tf_op jit(solution)/shard_map/all_to_all | solution.py:84
  58.6 3.5 %fusion.12 = f32[64,5120]{1,0:T(8,128)S(1)} fusion(bf16[64,512]{1,0:T(8,128)(2,1)S(1)} %reshape.44, bf16[512,5120]{1,0:T(8,128)(2,1)} %param.13), kind=kOutput, calls=%fused_computation.29 | convolution fusion | flops 335544320 | bytes 6619136 | tf_op jit(solution)/shard_map/dot_general | solution.py:85
  62.2 3.3 %all-to-all-done.2 = bf16[16,8,384]{2,1,0:T(8,128)(2,1)S(1)} async-done(((bf16[16,8,384]{2,1,0:T(8,128)(2,1)}), bf16[16,8,384]{2,1,0:T(8,128)(2,1)S(1)}, u32[]{:S(2)}, u32[]{:S(2)}) %all-to-all-start.2) | async-done | bytes 98336 | tf_op jit(solution)/shard_map/all_to_all | solution.py:84
  65.5 0.1 slice_bitcast_fusion
  65.6 0.1 reshape.46
  65.7 0.4 fusion.3
  66.1 12.8 %all_to_all.20 = bf16[8,8,5120]{2,1,0:T(8,128)(2,1)S(1)} all-to-all(bf16[8,8,5120]{2,1,0:T(8,128)(2,1)S(1)} %fusion.3), channel_id=1, replica_groups={{0,1,2,3,4,5,6,7},{8,9,10,11,12,13,14,15},{16,17,18,19,20,21,22,23},{24..., dimensions={0} | all-to-all | bytes 1310720 | tf_op jit(solution)/shard_map/all_to_all | solution.py:95
  78.9 0.1 convert_reduce_fusion
  79.1 2.8 %collective-permute-start.2 = (bf16[4,5120]{1,0:T(4,128)(2,1)S(1)}, bf16[4,5120]{1,0:T(4,128)(2,1)S(1)}, u32[]{:S(2)}, u32[]{:S(2)}) collective-permute-start(bf16[4,5120]{1,0:T(4,128)(2,1)S(1)} %select_convert_fusion), channel_id=1, source_target_pairs={{0,8},{1,9},{2,10},{3,11},{4,12},{5,13},{6,14},{7,15},{8,0},{9,1},... | collective-permute-start | bytes 122888 | tf_op jit(solution)/shard_map/ppermute | solution.py:50
  81.9 4.1 %collective-permute-done.2 = bf16[4,5120]{1,0:T(4,128)(2,1)S(1)} collective-permute-done((bf16[4,5120]{1,0:T(4,128)(2,1)S(1)}, bf16[4,5120]{1,0:T(4,128)(2,1)S(1)}, u32[]{:S(2)}, u32[]{:S(2)}) %collective-permute-start.2) | collective-permute-done | bytes 40992 | tf_op jit(solution)/shard_map/ppermute | solution.py:50
  86.0 0.7 add_convert_fusion
  (15 shorter events, 0.2 us)
Async XLA Ops:
  0.0 21.1 %copy-start = (bf16[4,8,128,128]{3,2,1,0:T(8,128)(2,1)S(1)}, bf16[4,8,128,128]{3,2,1,0:T(8,128)(2,1)}, u32[]{:S(2)}) copy-start(bf16[4,8,128,128]{3,2,1,0:T(8,128)(2,1)} %param.9) | copy-start | bytes 3145732
  0.0 22.8 %copy-start.1 = (bf16[4,8,128,128]{3,2,1,0:T(8,128)(2,1)S(1)}, bf16[4,8,128,128]{3,2,1,0:T(8,128)(2,1)}, u32[]{:S(2)}) copy-start(bf16[4,8,128,128]{3,2,1,0:T(8,128)(2,1)} %param.10) | copy-start | bytes 3145732
  1.5 31.6 %all-to-all-start = ((bf16[16,2,832]{2,1,0:T(2,128)(2,1)}), bf16[16,2,832]{2,1,0:T(2,128)(2,1)S(1)}, u32[]{:S(2)}, u32[]{:S(2)}) async-start(bf16[16,2,832]{2,1,0:T(2,128)(2,1)} %broadcast_in_dim.10), calls=%async_computation | async-start | bytes 114688 | tf_op jit(solution)/shard_map/all_to_all | solution.py:46
  33.1 12.9 %collective-permute-start = (bf16[32,832]{1,0:T(8,128)(2,1)S(1)}, bf16[32,832]{1,0:T(8,128)(2,1)S(1)}, u32[]{:S(2)}, u32[]{:S(2)}) collective-permute-start(bf16[32,832]{1,0:T(8,128)(2,1)S(1)} %reshape.41), channel_id=1, source_target_pairs={{0,32},{16,48},{32,0},{48,16},{64,96},{80,112},{96,64},{112,80},{1... | collective-permute-start | bytes 159752 | tf_op jit(solution)/shard_map/ppermute | solution.py:50
  40.0 13.0 %all-to-all-start.1 = ((bf16[16,4,512]{2,1,0:T(4,128)(2,1)}), bf16[16,4,512]{2,1,0:T(4,128)(2,1)S(1)}, u32[]{:S(2)}, u32[]{:S(2)}) async-start(bf16[16,4,512]{2,1,0:T(4,128)(2,1)} %bitcast.1), calls=%async_computation.1 | async-start | bytes 131072 | tf_op jit(solution)/shard_map/all_to_all | solution.py:76
  46.0 6.9 %collective-permute-start.1 = (bf16[64,832]{1,0:T(8,128)(2,1)S(1)}, bf16[64,832]{1,0:T(8,128)(2,1)S(1)}, u32[]{:S(2)}, u32[]{:S(2)}) collective-permute-start(bf16[64,832]{1,0:T(8,128)(2,1)S(1)} %pad_maximum_fusion), channel_id=1, source_target_pairs={{0,16},{16,0},{32,48},{48,32},{64,80},{80,64},{96,112},{112,96},{1... | collective-permute-start | bytes 319496 | tf_op jit(solution)/shard_map/ppermute | solution.py:50
  54.0 11.4 %all-to-all-start.2 = ((bf16[16,8,384]{2,1,0:T(8,128)(2,1)}), bf16[16,8,384]{2,1,0:T(8,128)(2,1)S(1)}, u32[]{:S(2)}, u32[]{:S(2)}) async-start(bf16[16,8,384]{2,1,0:T(8,128)(2,1)} %maximum_bitcast_fusion), calls=%async_computation.2 | async-start | bytes 196608 | tf_op jit(solution)/shard_map/all_to_all | solution.py:84
  58.6 3.5 %copy-start.2 = (bf16[4,5120]{1,0:T(4,128)(2,1)S(1)}, bf16[4,5120]{1,0:T(4,128)(2,1)}, u32[]{:S(2)}) copy-start(bf16[4,5120]{1,0:T(4,128)(2,1)} %param.12) | copy-start | bytes 122884
  79.1 6.9 %collective-permute-start.2 = (bf16[4,5120]{1,0:T(4,128)(2,1)S(1)}, bf16[4,5120]{1,0:T(4,128)(2,1)S(1)}, u32[]{:S(2)}, u32[]{:S(2)}) collective-permute-start(bf16[4,5120]{1,0:T(4,128)(2,1)S(1)} %select_convert_fusion), channel_id=1, source_target_pairs={{0,8},{1,9},{2,10},{3,11},{4,12},{5,13},{6,14},{7,15},{8,0},{9,1},... | collective-permute-start | bytes 122888 | tf_op jit(solution)/shard_map/ppermute | solution.py:50

commit v2 on v0

--- a/solution.py
+++ b/solution.py
@@ -79,14 +79,15 @@
     low_part = lax.dot_general(
         down, grouped, (((1,), (1,)), ((), ())), preferred_element_type=jnp.float32
     ).astype(jnp.bfloat16)
-    by_rank = jnp.concatenate([low_part, up], axis=1)
+    by_rank = jnp.concatenate([up, low_part], axis=1)
+    split = up.shape[1]
     by_rank = lax.all_to_all(by_rank.reshape(N_TENSOR, -1, by_rank.shape[1]), "tensor", 0, 0)
     partial_value = jnp.dot(grouped, output_weight, preferred_element_type=jnp.float32)
     residual, upper, by_rank = lax.optimization_barrier(
         (hidden.astype(jnp.float32), lax.axis_index("tensor") >= HALF, by_rank)
     )
-    low = jnp.sum(by_rank[:, :, : N_TENSOR * rows].astype(jnp.float32), axis=0)
-    up = by_rank[:, :, N_TENSOR * rows :].transpose(1, 0, 2).reshape(-1, width)
+    low = jnp.sum(by_rank[:, :, split:].astype(jnp.float32), axis=0)
+    up = by_rank[:, :, :split].transpose(1, 0, 2).reshape(-1, width)
     delta = lax.dot_general(
         low.astype(jnp.bfloat16), up, (((0,), (0,)), ((), ())), preferred_element_type=jnp.float32
     )

time: 87.2 us -> 87.2 us (level)
  no operation moved by 1% of the time
where the time goes in v2:
time: 87.2 us; the launch traced here: 86.6 us
  starting transfers between devices  41 us (47%)
  waiting for transfers between devices  20.6 us (24%)
  blocking collectives  12.8 us (15%)
  matrix products  6.08 us (7%)
  other arithmetic  4.19 us (5%)
  local copies, waits for them, and re-layouts  1.78 us (2%)
    all_to_all x1, starting transfers between devices, spread(): return lax.all_to_all(copies, axis, 0, 0, axis_index_groups=groups)  18.9 us
    all_to_all x1, blocking collectives, per_device(): lax.all_to_all(partial_value.reshape(HALF, 2 * rows, width), 'tensor', 0,...  12.8 us
    ppermute x3, starting transfers between devices, swap(): return lax.ppermute(block, axis, [(i, i ^ bit) for i in range(count)])  11.5 us
    all_to_all x1, waiting for transfers between devices, spread(): return lax.all_to_all(copies, axis, 0, 0, axis_index_groups=groups)  8.14 us
    all_to_all x1, starting transfers between devices, per_device(): lax.all_to_all(blocks, 'tensor', 0, 0, axis_index_groups=PLACE_GROUPS)  6.02 us
    all_to_all x1, waiting for transfers between devices, per_device(): lax.all_to_all(blocks, 'tensor', 0, 0, axis_index_groups=PLACE_GROUPS)  4.97 us
    all_to_all x1, starting transfers between devices, per_device(): lax.all_to_all(by_rank.reshape(N_TENSOR, -1, by_rank.shape[1]), 'tensor',...  4.6 us
    ppermute x3, waiting for transfers between devices, swap(): return lax.ppermute(block, axis, [(i, i ^ bit) for i in range(count)])  4.16 us
  transfers between devices with their start and end apart: 6, of which 4 were waited for; matrix products, arithmetic and copies ran while one was open for 9% of the time, Pallas kernels for 0%

profile of v2, /device:TPU:8, one launch (start us, length us, event | category | flops | bytes accessed | tf_op | source)
XLA Modules:
  0.0 86.6 jit_solution(8507405767228486470)
XLA Ops:
  0.0 0.9 pad_maximum_fusion.1
  0.9 0.6 broadcast_in_dim.10
  1.5 18.9 %all-to-all-start = ((bf16[16,2,832]{2,1,0:T(2,128)(2,1)}), bf16[16,2,832]{2,1,0:T(2,128)(2,1)S(1)}, u32[]{:S(2)}, u32[]{:S(2)}) async-start(bf16[16,2,832]{2,1,0:T(2,128)(2,1)} %broadcast_in_dim.10), calls=%async_computation | async-start | bytes 114688 | tf_op jit(solution)/shard_map/all_to_all | solution.py:46
  20.4 0.7 iota_compare_fusion
  21.1 0.8 convert_element_type.29
  21.9 1.5 %fusion.6 = f32[4,8,8,128]{3,2,1,0:T(8,128)S(1)} fusion(bf16[4,8,128,128]{3,2,1,0:T(8,128)(2,1)S(1)} %copy-done, bf16[1,4,64,128]{3,1,2,0:T(4,128)(2,1)} %bitcast.25, pred[4,128]{1,0:T(4,128)(4,1)S(1)} %iota_compare_fusion), kind=kOutput, calls=%fused_computation.9 | convolution fusion | flops 8454144 | bytes 1245696 | tf_op jit(solution)/shard_map/rkgd,rksd->rkgs/dot_general | solution.py:28
  23.4 0.2 fusion.11
  23.6 0.6 convolution_convert_fusion
  24.2 0.1 reshape_reshape.3
  24.3 0.7 copy.12
  24.9 8.1 %all-to-all-done = bf16[16,2,832]{2,1,0:T(2,128)(2,1)S(1)} async-done(((bf16[16,2,832]{2,1,0:T(2,128)(2,1)}), bf16[16,2,832]{2,1,0:T(2,128)(2,1)S(1)}, u32[]{:S(2)}, u32[]{:S(2)}) %all-to-all-start) | async-done | bytes 53280 | tf_op jit(solution)/shard_map/all_to_all | solution.py:46
  33.1 0.1 reshape.41
  33.1 6.8 %collective-permute-start = (bf16[32,832]{1,0:T(8,128)(2,1)S(1)}, bf16[32,832]{1,0:T(8,128)(2,1)S(1)}, u32[]{:S(2)}, u32[]{:S(2)}) collective-permute-start(bf16[32,832]{1,0:T(8,128)(2,1)S(1)} %reshape.41), channel_id=1, source_target_pairs={{0,32},{16,48},{32,0},{48,16},{64,96},{80,112},{96,64},{112,80},{1... | collective-permute-start | bytes 159752 | tf_op jit(solution)/shard_map/ppermute | solution.py:50
  40.0 6.0 %all-to-all-start.1 = ((bf16[16,4,512]{2,1,0:T(4,128)(2,1)}), bf16[16,4,512]{2,1,0:T(4,128)(2,1)S(1)}, u32[]{:S(2)}, u32[]{:S(2)}) async-start(bf16[16,4,512]{2,1,0:T(4,128)(2,1)} %bitcast.1), calls=%async_computation.1 | async-start | bytes 131072 | tf_op jit(solution)/shard_map/all_to_all | solution.py:76
  46.0 0.0 collective-permute-done
  46.0 1.9 %collective-permute-start.1 = (bf16[64,832]{1,0:T(8,128)(2,1)S(1)}, bf16[64,832]{1,0:T(8,128)(2,1)S(1)}, u32[]{:S(2)}, u32[]{:S(2)}) collective-permute-start(bf16[64,832]{1,0:T(8,128)(2,1)S(1)} %pad_maximum_fusion), channel_id=1, source_target_pairs={{0,16},{16,0},{32,48},{48,32},{64,80},{80,64},{96,112},{112,96},{1... | collective-permute-start | bytes 319496 | tf_op jit(solution)/shard_map/ppermute | solution.py:50
  48.0 5.0 %all-to-all-done.1 = bf16[16,4,512]{2,1,0:T(4,128)(2,1)S(1)} async-done(((bf16[16,4,512]{2,1,0:T(4,128)(2,1)}), bf16[16,4,512]{2,1,0:T(4,128)(2,1)S(1)}, u32[]{:S(2)}, u32[]{:S(2)}) %all-to-all-start.1) | async-done | bytes 65568 | tf_op jit(solution)/shard_map/all_to_all | solution.py:76
  53.0 0.0 collective-permute-done.1
  53.0 0.2 convolution_convert_fusion.1
  53.2 0.1 copy.13
  53.3 0.7 maximum_bitcast_fusion
  54.0 4.6 %all-to-all-start.2 = ((bf16[16,8,384]{2,1,0:T(8,128)(2,1)}), bf16[16,8,384]{2,1,0:T(8,128)(2,1)S(1)}, u32[]{:S(2)}, u32[]{:S(2)}) async-start(bf16[16,8,384]{2,1,0:T(8,128)(2,1)} %maximum_bitcast_fusion), calls=%async_computation.2 | async-start | bytes 196608 | tf_op jit(solution)/shard_map/all_to_all | solution.py:84
  58.6 3.5 %fusion.12 = f32[64,5120]{1,0:T(8,128)S(1)} fusion(bf16[64,512]{1,0:T(8,128)(2,1)S(1)} %reshape.44, bf16[512,5120]{1,0:T(8,128)(2,1)} %param.13), kind=kOutput, calls=%fused_computation.29 | convolution fusion | flops 335544320 | bytes 6619136 | tf_op jit(solution)/shard_map/dot_general | solution.py:85
  62.1 3.3 %all-to-all-done.2 = bf16[16,8,384]{2,1,0:T(8,128)(2,1)S(1)} async-done(((bf16[16,8,384]{2,1,0:T(8,128)(2,1)}), bf16[16,8,384]{2,1,0:T(8,128)(2,1)S(1)}, u32[]{:S(2)}, u32[]{:S(2)}) %all-to-all-start.2) | async-done | bytes 98336 | tf_op jit(solution)/shard_map/all_to_all | solution.py:84
  65.4 0.1 slice_reduce_fusion
  65.6 0.1 reshape.46
  65.7 0.4 fusion.3
  66.1 12.8 %all_to_all.20 = bf16[8,8,5120]{2,1,0:T(8,128)(2,1)S(1)} all-to-all(bf16[8,8,5120]{2,1,0:T(8,128)(2,1)S(1)} %fusion.3), channel_id=1, replica_groups={{0,1,2,3,4,5,6,7},{8,9,10,11,12,13,14,15},{16,17,18,19,20,21,22,23},{24..., dimensions={0} | all-to-all | bytes 1310720 | tf_op jit(solution)/shard_map/all_to_all | solution.py:95
  78.9 0.1 convert_reduce_fusion
  79.0 2.7 %collective-permute-start.2 = (bf16[4,5120]{1,0:T(4,128)(2,1)S(1)}, bf16[4,5120]{1,0:T(4,128)(2,1)S(1)}, u32[]{:S(2)}, u32[]{:S(2)}) collective-permute-start(bf16[4,5120]{1,0:T(4,128)(2,1)S(1)} %select_convert_fusion), channel_id=1, source_target_pairs={{0,8},{1,9},{2,10},{3,11},{4,12},{5,13},{6,14},{7,15},{8,0},{9,1},... | collective-permute-start | bytes 122888 | tf_op jit(solution)/shard_map/ppermute | solution.py:50
  81.8 4.2 %collective-permute-done.2 = bf16[4,5120]{1,0:T(4,128)(2,1)S(1)} collective-permute-done((bf16[4,5120]{1,0:T(4,128)(2,1)S(1)}, bf16[4,5120]{1,0:T(4,128)(2,1)S(1)}, u32[]{:S(2)}, u32[]{:S(2)}) %collective-permute-start.2) | collective-permute-done | bytes 40992 | tf_op jit(solution)/shard_map/ppermute | solution.py:50
  85.9 0.7 add_convert_fusion
  (13 shorter events, 0.2 us)
Async XLA Ops:
  0.0 21.9 %copy-start = (bf16[4,8,128,128]{3,2,1,0:T(8,128)(2,1)S(1)}, bf16[4,8,128,128]{3,2,1,0:T(8,128)(2,1)}, u32[]{:S(2)}) copy-start(bf16[4,8,128,128]{3,2,1,0:T(8,128)(2,1)} %param.9) | copy-start | bytes 3145732
  0.0 23.6 %copy-start.1 = (bf16[4,8,128,128]{3,2,1,0:T(8,128)(2,1)S(1)}, bf16[4,8,128,128]{3,2,1,0:T(8,128)(2,1)}, u32[]{:S(2)}) copy-start(bf16[4,8,128,128]{3,2,1,0:T(8,128)(2,1)} %param.10) | copy-start | bytes 3145732
  1.5 31.6 %all-to-all-start = ((bf16[16,2,832]{2,1,0:T(2,128)(2,1)}), bf16[16,2,832]{2,1,0:T(2,128)(2,1)S(1)}, u32[]{:S(2)}, u32[]{:S(2)}) async-start(bf16[16,2,832]{2,1,0:T(2,128)(2,1)} %broadcast_in_dim.10), calls=%async_computation | async-start | bytes 114688 | tf_op jit(solution)/shard_map/all_to_all | solution.py:46
  33.1 12.9 %collective-permute-start = (bf16[32,832]{1,0:T(8,128)(2,1)S(1)}, bf16[32,832]{1,0:T(8,128)(2,1)S(1)}, u32[]{:S(2)}, u32[]{:S(2)}) collective-permute-start(bf16[32,832]{1,0:T(8,128)(2,1)S(1)} %reshape.41), channel_id=1, source_target_pairs={{0,32},{16,48},{32,0},{48,16},{64,96},{80,112},{96,64},{112,80},{1... | collective-permute-start | bytes 159752 | tf_op jit(solution)/shard_map/ppermute | solution.py:50
  40.0 13.0 %all-to-all-start.1 = ((bf16[16,4,512]{2,1,0:T(4,128)(2,1)}), bf16[16,4,512]{2,1,0:T(4,128)(2,1)S(1)}, u32[]{:S(2)}, u32[]{:S(2)}) async-start(bf16[16,4,512]{2,1,0:T(4,128)(2,1)} %bitcast.1), calls=%async_computation.1 | async-start | bytes 131072 | tf_op jit(solution)/shard_map/all_to_all | solution.py:76
  46.0 6.9 %collective-permute-start.1 = (bf16[64,832]{1,0:T(8,128)(2,1)S(1)}, bf16[64,832]{1,0:T(8,128)(2,1)S(1)}, u32[]{:S(2)}, u32[]{:S(2)}) collective-permute-start(bf16[64,832]{1,0:T(8,128)(2,1)S(1)} %pad_maximum_fusion), channel_id=1, source_target_pairs={{0,16},{16,0},{32,48},{48,32},{64,80},{80,64},{96,112},{112,96},{1... | collective-permute-start | bytes 319496 | tf_op jit(solution)/shard_map/ppermute | solution.py:50
  54.0 11.4 %all-to-all-start.2 = ((bf16[16,8,384]{2,1,0:T(8,128)(2,1)}), bf16[16,8,384]{2,1,0:T(8,128)(2,1)S(1)}, u32[]{:S(2)}, u32[]{:S(2)}) async-start(bf16[16,8,384]{2,1,0:T(8,128)(2,1)} %maximum_bitcast_fusion), calls=%async_computation.2 | async-start | bytes 196608 | tf_op jit(solution)/shard_map/all_to_all | solution.py:84
  79.0 6.9 %collective-permute-start.2 = (bf16[4,5120]{1,0:T(4,128)(2,1)S(1)}, bf16[4,5120]{1,0:T(4,128)(2,1)S(1)}, u32[]{:S(2)}, u32[]{:S(2)}) collective-permute-start(bf16[4,5120]{1,0:T(4,128)(2,1)S(1)} %select_convert_fusion), channel_id=1, source_target_pairs={{0,8},{1,9},{2,10},{3,11},{4,12},{5,13},{6,14},{7,15},{8,0},{9,1},... | collective-permute-start | bytes 122888 | tf_op jit(solution)/shard_map/ppermute | solution.py:50
